TPU v7x, 256 devices: a whole 4x4x8 slice. The times are simulated.
256 devices in a mesh: dp: 4 (over x), expert: 64 (over y, z, core).
Axes of the slice: x: 4, y: 4, z: 8, core: 2. Of those that a mesh axis runs over, the one named last changes fastest.
Arguments:
- saved_input: bfloat16 [8192, 2048], P(('dp', 'expert')), may hold values from -6 to 6
- output_grad: bfloat16 [8192, 2048], P(('dp', 'expert')), may hold values from -6 to 6
- route_probs: float32 [8192, 8], P(('dp', 'expert')), may hold values from 0.02 to 0.4
- expert_choice: int32 [8192, 8], P(('dp', 'expert')), may hold values from 0 to 127, all different within a row; in each aligned block of 32 rows (0 to 31, 32 to 63, ...) at most 3 rows name the same one
- slot_expert: int32 [4, 64], replicated, may hold values from 0 to 127, as said below
- frozen_gate: bfloat16 [256, 2048, 768], P(('dp', 'expert')), as said below
- frozen_up: bfloat16 [256, 2048, 768], P(('dp', 'expert')), as said below
- frozen_down: bfloat16 [256, 768, 2048], P(('dp', 'expert')), as said below
- adapter_in: float32 [128, 64, 768], P('expert', 'dp'), may hold values from -0.21875 to 0.21875
- adapter_out: float32 [128, 64, 2048], P('expert', 'dp'), may hold values from -0.125 to 0.125
- moment_in: float32 [128, 64, 768], P('expert', 'dp'), may hold values from -3 to 3
- moment_out: float32 [128, 64, 2048], P('expert', 'dp'), may hold values from -3 to 3
- second_in: float32 [128, 64, 768], P('expert', 'dp'), may hold values from 0.01 to 1
- second_out: float32 [128, 64, 2048], P('expert', 'dp'), may hold values from 0.01 to 1
Outputs:
- input_grad: bfloat16 [8192, 2048], P(('dp', 'expert'))
- step_in: float32 [128, 64, 768], P('expert', 'dp')
- step_out: float32 [128, 64, 2048], P('expert', 'dp')
- momentum_in: float32 [128, 64, 768], P('expert', 'dp')
- momentum_out: float32 [128, 64, 2048], P('expert', 'dp')
- variance_in: float32 [128, 64, 768], P('expert', 'dp')
- variance_out: float32 [128, 64, 2048], P('expert', 'dp')
- replica_in: bfloat16 [256, 64, 768], P(('dp', 'expert'))
- replica_out: bfloat16 [256, 64, 2048], P(('dp', 'expert'))
Inputs may be any that keep to these rules, and one draw needn't show every extreme that they name: `expert_choice`: among the rows of one device no expert is named more than 3 times. `slot_expert`: the slots of index j of the expert axis host only experts 2 * j to 2 * j + 1, and each of these at least once. `frozen_gate`: slots that host the same expert hold the same frozen weights. `frozen_up`: slots that host the same expert hold the same frozen weights. `frozen_down`: slots that host the same expert hold the same frozen weights.
All inputs are finite; a program needn't handle non-finite values.
Results may differ from a plain program's by a relative error of at most 0.012.
Values may be sent and summed in bfloat16 or wider, within the bound.
A program may use at most 128 MiB of HBM per device.

v0:
```python
import jax
import jax.numpy as jnp
from jax import lax
from jax.sharding import PartitionSpec as P

STEP = 100
adapter_scale_factor = 2.0
beta_one = 0.9
beta_two = 0.999
decay_rate = 0.01
adam_eps = 1e-08


def contract_product(left, right, left_dim, right_dim):
    return lax.dot_general(
        left, right, (((left_dim,), (right_dim,)), ((), ())), preferred_element_type=jnp.float32
    )


def route_rows(choice_flat, slot_expert, source, local_experts):
    column = choice_flat // local_experts
    hosted = (jnp.take(slot_expert, column, axis=1) == choice_flat[None, :]).astype(jnp.int32)
    counts = jnp.sum(hosted, axis=0)
    picked = source % counts
    running = jnp.cumsum(hosted, axis=0) - 1
    chosen = hosted * (running == picked[None, :]).astype(jnp.int32)
    dp_ids = jnp.arange(hosted.shape[0], dtype=jnp.int32)
    dest_row = jnp.sum(chosen * dp_ids[:, None], axis=0)
    row_ids = jnp.arange(choice_flat.shape[0], dtype=jnp.int32)
    earlier = (choice_flat[None, :] == choice_flat[:, None]) & (row_ids[None, :] < row_ids[:, None])
    rank = jnp.sum(earlier.astype(jnp.int32), axis=1)
    return (dest_row, column, rank)


def pack_rows(saved_input, scaled, position, buffer_size, top_count, shape_out):
    row_count = scaled.shape[0]
    row_ids = jnp.arange(row_count, dtype=jnp.int32)
    filler = jnp.full((buffer_size,), row_count, jnp.int32).at[position].set(row_ids)
    send_input = jnp.take(saved_input, filler // top_count, axis=0, mode="fill", fill_value=0)
    send_grad = jnp.take(scaled, filler, axis=0, mode="fill", fill_value=0)
    return (send_input.reshape(shape_out), send_grad.reshape(shape_out))


def adamw(param, grad, first, second):
    first_new = beta_one * first + (1.0 - beta_one) * grad
    second_new = beta_two * second + (1.0 - beta_two) * grad * grad
    corr_one = 1.0 - beta_one**STEP
    corr_two = 1.0 - beta_two**STEP
    step_dir = (
        first_new / corr_one / (jnp.sqrt(second_new / corr_two) + adam_eps) + decay_rate * param
    )
    return (step_dir, first_new, second_new)


def per_device(
    saved_input,
    output_grad,
    route_probs,
    expert_choice,
    slot_expert,
    frozen_gate,
    frozen_up,
    frozen_down,
    adapter_in,
    adapter_out,
    moment_in,
    moment_out,
    second_in,
    second_out,
):
    dp_count = lax.axis_size("dp")
    expert_count = lax.axis_size("expert")
    dp_index = lax.axis_index("dp")
    column_index = lax.axis_index("expert")
    local_experts = adapter_in.shape[0]
    token_count, top_count = expert_choice.shape
    width = saved_input.shape[1]
    row_count = token_count * top_count
    capacity = max(2, -(-3 * row_count // (2 * local_experts * expert_count)))
    buffer_size = dp_count * expert_count * capacity
    source = dp_index * expert_count + column_index
    choice_flat = expert_choice.reshape(row_count)
    dest_row, column, rank = route_rows(choice_flat, slot_expert, source, local_experts)
    scaled = (
        (route_probs[:, :, None] * output_grad[:, None, :].astype(jnp.float32))
        .astype(jnp.bfloat16)
        .reshape(row_count, width)
    )
    slot_shape = (dp_count, expert_count, capacity, width)
    position = (dest_row * expert_count + column) * capacity + rank
    send_input, send_grad = pack_rows(
        saved_input, scaled, position, buffer_size, top_count, slot_shape
    )
    arrived_input, arrived_grad = (
        lax.all_to_all(
            lax.all_to_all(send_input, "dp", split_axis=0, concat_axis=0, tiled=True),
            "expert",
            split_axis=1,
            concat_axis=1,
            tiled=True,
        ),
        lax.all_to_all(
            lax.all_to_all(send_grad, "dp", split_axis=0, concat_axis=0, tiled=True),
            "expert",
            split_axis=1,
            concat_axis=1,
            tiled=True,
        ),
    )
    fetched_in, fetched_out = (
        lax.all_gather(adapter_in.astype(jnp.bfloat16), "dp", axis=1, tiled=True),
        lax.all_gather(adapter_out.astype(jnp.bfloat16), "dp", axis=1, tiled=True),
    )
    hosted_local = slot_expert[dp_index, column_index] - local_experts * column_index
    owned_input = lax.dynamic_index_in_dim(fetched_in, hosted_local, 0, keepdims=False)
    own_out = lax.dynamic_index_in_dim(fetched_out, hosted_local, 0, keepdims=False)
    buffer_rows = arrived_input.reshape(buffer_size, width)
    gradient_row_block = arrived_grad.reshape(buffer_size, width)
    gate_weight = frozen_gate[0]
    up_weight = frozen_up[0]
    down_weight = frozen_down[0]
    gate_pre = jnp.dot(buffer_rows, gate_weight, preferred_element_type=jnp.float32)
    up_pre = jnp.dot(buffer_rows, up_weight, preferred_element_type=jnp.float32)
    sigmoid_gate = jax.nn.sigmoid(gate_pre)
    hidden_state = (gate_pre * sigmoid_gate * up_pre).astype(jnp.bfloat16)
    low_rank_input = contract_product(hidden_state, owned_input, 1, 1).astype(jnp.bfloat16)
    low_rank_gradient = contract_product(gradient_row_block, own_out, 1, 1).astype(jnp.bfloat16)
    hidden_gradient = contract_product(gradient_row_block, down_weight, 1, 1)
    hidden_gradient = hidden_gradient + adapter_scale_factor * jnp.dot(
        low_rank_gradient, owned_input, preferred_element_type=jnp.float32
    )
    up_grad = (hidden_gradient * gate_pre * sigmoid_gate).astype(jnp.bfloat16)
    gate_grad = (
        hidden_gradient * up_pre * sigmoid_gate * (1.0 + gate_pre * (1.0 - sigmoid_gate))
    ).astype(jnp.bfloat16)
    back_rows = (
        contract_product(gate_grad, gate_weight, 1, 1) + contract_product(up_grad, up_weight, 1, 1)
    ).astype(jnp.bfloat16)
    incoming_gradient = adapter_scale_factor * contract_product(
        low_rank_gradient, hidden_state, 0, 0
    )
    outgoing_gradient = adapter_scale_factor * contract_product(
        low_rank_input, gradient_row_block, 0, 0
    )
    back_block = back_rows.reshape(dp_count, expert_count, capacity, width)
    returned = lax.all_to_all(
        lax.all_to_all(back_block, "dp", split_axis=0, concat_axis=0, tiled=True),
        "expert",
        split_axis=1,
        concat_axis=1,
        tiled=True,
    )
    per_row = jnp.take(returned.reshape(buffer_size, width), position, axis=0)
    input_grad = jnp.sum(
        per_row.reshape(token_count, top_count, width).astype(jnp.float32), axis=1
    ).astype(jnp.bfloat16)
    selector = (jnp.arange(local_experts, dtype=jnp.int32) == hosted_local).astype(jnp.float32)
    placed_in = selector[:, None, None] * incoming_gradient[None, :, :]
    placed_out = selector[:, None, None] * outgoing_gradient[None, :, :]
    summed_in, summed_out = (
        lax.psum_scatter(placed_in, "dp", scatter_dimension=1, tiled=True),
        lax.psum_scatter(placed_out, "dp", scatter_dimension=1, tiled=True),
    )
    step_in, momentum_in, variance_in = adamw(adapter_in, summed_in, moment_in, second_in)
    step_out, momentum_out, variance_out = adamw(adapter_out, summed_out, moment_out, second_out)
    copied_in, copied_out = (
        lax.all_gather(step_in.astype(jnp.bfloat16), "dp", axis=1, tiled=True),
        lax.all_gather(step_out.astype(jnp.bfloat16), "dp", axis=1, tiled=True),
    )
    replica_in = lax.dynamic_index_in_dim(copied_in, hosted_local, 0, keepdims=True)
    replica_out = lax.dynamic_index_in_dim(copied_out, hosted_local, 0, keepdims=True)
    return (
        input_grad,
        step_in,
        step_out,
        momentum_in,
        momentum_out,
        variance_in,
        variance_out,
        replica_in,
        replica_out,
    )


def solution(mesh):
    return jax.shard_map(
        per_device,
        mesh=mesh,
        in_specs=(
            P(("dp", "expert"), None),
            P(("dp", "expert"), None),
            P(("dp", "expert"), None),
            P(("dp", "expert"), None),
            P(),
            P(("dp", "expert"), None, None),
            P(("dp", "expert"), None, None),
            P(("dp", "expert"), None, None),
            P("expert", "dp", None),
            P("expert", "dp", None),
            P("expert", "dp", None),
            P("expert", "dp", None),
            P("expert", "dp", None),
            P("expert", "dp", None),
        ),
        out_specs=(
            P(("dp", "expert"), None),
            P("expert", "dp", None),
            P("expert", "dp", None),
            P("expert", "dp", None),
            P("expert", "dp", None),
            P("expert", "dp", None),
            P("expert", "dp", None),
            P(("dp", "expert"), None, None),
            P(("dp", "expert"), None, None),
        ),
        check_vma=False,
    )
```

profile of v0, /device:TPU:1, one launch (start us, length us, event | category | flops | bytes accessed | tf_op | source)
XLA Modules:
  0.0 540.5 jit_solution(13556978153045774076)
XLA Ops:
  7.2 0.9 copy.50
  8.3 0.7 convert_reduce_fusion
  9.7 0.8 copy.52
  10.4 0.7 gather_fusion
  12.0 0.7 and_select_fusion.1
  12.9 1.0 multiply_reduce_fusion
  13.9 0.7 compare_select_fusion.2
  15.1 1.4 scatter_custom_fusion
  16.6 4.3 gather_fusion.2
  20.8 9.1 %gather.26 = bf16[4,64,3,2048]{3,2,1,0:T(4,128)(2,1)} reshape(bf16[768,2048]{1,0:T(8,128)(2,1)} %gather_fusion.2) | data formatting | bytes 6291456 | tf_op jit(solution)/shard_map/jit(_take)/gather | solution.py:39
  30.2 4.1 broadcast_select_fusion
  34.3 4.0 copy.61
  38.3 5.2 all-to-all-start.2
  43.7 0.9 convert_element_type.56
  44.9 1.2 fusion.9
  46.0 8.5 %gather_fusion.1 = bf16[768,2048]{1,0:T(8,128)(2,1)} fusion(bf16[256,2048]{1,0:T(8,128)(2,1)} %fusion.9, s32[1024]{0:T(1024)S(1)} %pad_clamp_fusion.2), kind=kCustom, calls=%fused_computation.1 | custom fusion | bytes 6294528 | tf_op jit(solution)/shard_map/jit(_take)/gather | solution.py:40
  54.6 9.1 %gather.24 = bf16[4,64,3,2048]{3,2,1,0:T(4,128)(2,1)} reshape(bf16[768,2048]{1,0:T(8,128)(2,1)} %gather_fusion.1) | data formatting | bytes 6291456 | tf_op jit(solution)/shard_map/jit(_take)/gather | solution.py:40
  63.6 4.1 broadcast_select_fusion.1
  67.8 4.1 copy.58
  71.8 7.2 %all-to-all-done.2 = bf16[4,64,3,2048]{3,1,2,0:T(8,128)(2,1)} async-done(((bf16[4,64,3,2048]{3,1,2,0:T(8,128)(2,1)}), bf16[4,64,3,2048]{3,1,2,0:T(8,128)(2,1)}, u32[]{:S(2)}, u32[]{:S(2)}) %all-to-all-start.2) | async-done | bytes 3145760 | tf_op jit(solution)/shard_map/all_to_all | solution.py:96
  79.0 4.7 all-to-all-start
  83.6 6.1 %copy.62 = bf16[4,64,3,2048]{3,0,2,1:T(4,128)(2,1)} copy(bf16[4,64,3,2048]{3,1,2,0:T(8,128)(2,1)} %all-to-all-done.2) | data formatting | bytes 6291456 | tf_op jit(solution)/shard_map/all_to_all | solution.py:96
  89.7 28.1 %all-to-all-done = bf16[4,64,3,2048]{3,1,2,0:T(8,128)(2,1)} async-done(((bf16[4,64,3,2048]{3,1,2,0:T(8,128)(2,1)}), bf16[4,64,3,2048]{3,1,2,0:T(8,128)(2,1)}, u32[]{:S(2)}, u32[]{:S(2)}) %all-to-all-start) | async-done | bytes 3145760 | tf_op jit(solution)/shard_map/all_to_all | solution.py:103
  117.8 19.1 %all-to-all-start.3 = ((bf16[4,64,3,2048]{3,0,2,1:T(4,128)(2,1)}), bf16[4,64,3,2048]{3,0,2,1:T(4,128)(2,1)}, u32[]{:S(2)}, u32[]{:S(2)}) async-start(bf16[4,64,3,2048]{3,0,2,1:T(4,128)(2,1)} %copy.62), calls=%async_computation.3 | async-start | bytes 6291456 | tf_op jit(solution)/shard_map/all_to_all | solution.py:95
  136.8 6.0 %copy.59 = bf16[4,64,3,2048]{3,0,2,1:T(4,128)(2,1)} copy(bf16[4,64,3,2048]{3,1,2,0:T(8,128)(2,1)} %all-to-all-done) | data formatting | bytes 6291456 | tf_op jit(solution)/shard_map/all_to_all | solution.py:103
  142.8 67.2 %all-to-all-done.3 = bf16[4,64,3,2048]{3,0,2,1:T(4,128)(2,1)} async-done(((bf16[4,64,3,2048]{3,0,2,1:T(4,128)(2,1)}), bf16[4,64,3,2048]{3,0,2,1:T(4,128)(2,1)}, u32[]{:S(2)}, u32[]{:S(2)}) %all-to-all-start.3) | async-done | bytes 3145760 | tf_op jit(solution)/shard_map/all_to_all | solution.py:95
  210.1 6.3 %all-to-all-start.1 = ((bf16[4,64,3,2048]{3,0,2,1:T(4,128)(2,1)}), bf16[4,64,3,2048]{3,0,2,1:T(4,128)(2,1)}, u32[]{:S(2)}, u32[]{:S(2)}) async-start(bf16[4,64,3,2048]{3,0,2,1:T(4,128)(2,1)} %copy.59), calls=%async_computation.1 | async-start | bytes 6291456 | tf_op jit(solution)/shard_map/all_to_all | solution.py:102
  216.4 1.3 dynamic_slice.19
  218.4 10.4 %all_gather.13 = bf16[2,64,768]{2,1,0:T(8,128)(2,1)S(1)} all-gather(bf16[2,16,768]{2,1,0:T(8,128)(2,1)S(1)} %convert_element_type.60), channel_id=1, replica_groups=mesh['dp'=4,'expert'=64] {'dp'}, dimensions={1}, use_global_device_ids=true | all-gather | bytes 245760 | tf_op jit(solution)/shard_map/all_gather | solution.py:111
  228.8 6.5 %copy.63 = bf16[4,64,3,2048]{3,2,1,0:T(4,128)(2,1)} copy(bf16[4,64,3,2048]{3,0,2,1:T(4,128)(2,1)} %all-to-all-done.3) | data formatting | bytes 6291456 | tf_op jit(solution)/shard_map/all_to_all | solution.py:95
  235.4 9.0 %reshape.237 = bf16[768,2048]{1,0:T(8,128)(2,1)} reshape(bf16[4,64,3,2048]{3,2,1,0:T(4,128)(2,1)} %copy.63) | data formatting | bytes 6291456 | tf_op jit(solution)/shard_map/reshape | solution.py:117
  244.3 45.5 %all-to-all-done.1 = bf16[4,64,3,2048]{3,0,2,1:T(4,128)(2,1)} async-done(((bf16[4,64,3,2048]{3,0,2,1:T(4,128)(2,1)}), bf16[4,64,3,2048]{3,0,2,1:T(4,128)(2,1)}, u32[]{:S(2)}, u32[]{:S(2)}) %all-to-all-start.1) | async-done | bytes 3145760 | tf_op jit(solution)/shard_map/all_to_all | solution.py:102
  289.8 6.5 %copy.60 = bf16[4,64,3,2048]{3,2,1,0:T(4,128)(2,1)} copy(bf16[4,64,3,2048]{3,0,2,1:T(4,128)(2,1)} %all-to-all-done.1) | data formatting | bytes 6291456 | tf_op jit(solution)/shard_map/all_to_all | solution.py:102
  296.3 8.8 %reshape.236 = bf16[768,2048]{1,0:T(8,128)(2,1)} reshape(bf16[4,64,3,2048]{3,2,1,0:T(4,128)(2,1)} %copy.60) | data formatting | bytes 6291456 | tf_op jit(solution)/shard_map/reshape | solution.py:118
  305.2 5.6 %fusion.2 = f32[768,768]{1,0:T(8,128)S(1)} fusion(bf16[768,2048]{1,0:T(8,128)(2,1)} %reshape.237, bf16[1,2048,768]{2,1,0:T(8,128)(2,1)} %param.19), kind=kOutput, calls=%fused_computation.10 | convolution fusion | flops 2415919104 | bytes 8650752 | tf_op jit(solution)/shard_map/dot_general | solution.py:122
  310.8 4.5 multiply_convert_fusion
  315.3 4.2 convolution_multiply_fusion
  319.5 2.2 broadcast_multiply_fusion
  321.8 6.9 %fusion.7 = f32[768,768]{1,0:T(8,128)} fusion(bf16[768,2048]{1,0:T(8,128)(2,1)} %reshape.236, bf16[1,768,2048]{2,1,0:T(8,128)(2,1)} %param.21), kind=kOutput, calls=%fused_computation.15 | convolution fusion | flops 2415919104 | bytes 8650752 | tf_op jit(solution)/shard_map/dot_general | solution.py:15
  328.7 12.9 %reduce-scatter.5.cloned.1.call-done = f32[2,16,2048]{2,1,0:T(8,128)} async-done(((f32[2,64,2048]{2,1,0:T(8,128)}), f32[2,16,2048]{2,1,0:T(8,128)}) %reduce-scatter.5.cloned.1.call-update) | async-done | bytes 262160 | tf_op jit(solution)/shard_map/reduce_scatter | solution.py:162
  341.6 2.3 fusion.39
  343.9 11.2 %all_gather.12 = bf16[2,64,2048]{2,1,0:T(8,128)(2,1)S(1)} all-gather(bf16[2,16,2048]{2,1,0:T(8,128)(2,1)S(1)} %get-tuple-element.23), channel_id=1, replica_groups=mesh['dp'=4,'expert'=64] {'dp'}, dimensions={1}, use_global_device_ids=true | all-gather | bytes 655360 | tf_op jit(solution)/shard_map/all_gather | solution.py:112
  355.1 3.1 convolution_convert_fusion.1
  358.7 1.4 copy-done.15
  360.1 3.3 fusion
  363.5 4.1 add_convert_fusion
  367.5 9.1 %reshape.238 = bf16[4,64,3,2048]{3,2,1,0:T(4,128)(2,1)} reshape(bf16[768,2048]{1,0:T(8,128)(2,1)} %add_convert_fusion) | data formatting | bytes 6291456 | tf_op jit(solution)/shard_map/reshape | solution.py:145
  376.6 4.5 copy.64
  381.1 36.2 %all_to_all.30 = bf16[4,64,3,2048]{3,1,2,0:T(8,128)(2,1)S(1)} all-to-all(bf16[4,64,3,2048]{3,1,2,0:T(8,128)(2,1)S(1)} %copy.64), channel_id=1, replica_groups=mesh['dp'=4,'expert'=64] {'dp'}, dimensions={0} | all-to-all | bytes 6291456 | tf_op jit(solution)/shard_map/all_to_all | solution.py:147
  417.3 4.1 copy.65
  421.4 15.0 %all-to-all-start.5 = ((bf16[4,64,3,2048]{3,0,2,1:T(4,128)(2,1)}), bf16[4,64,3,2048]{3,0,2,1:T(4,128)(2,1)}, u32[]{:S(2)}, u32[]{:S(2)}) async-start(bf16[4,64,3,2048]{3,0,2,1:T(4,128)(2,1)} %copy.65), calls=%async_computation.5 | async-start | bytes 6291456 | tf_op jit(solution)/shard_map/all_to_all | solution.py:146
  436.4 1.6 convolution_multiply_fusion.1
  438.0 0.9 broadcast_multiply_fusion.1
  439.2 11.1 %all_gather.15 = bf16[2,64,2048]{2,1,0:T(8,128)(2,1)S(1)} all-gather(bf16[2,16,2048]{2,1,0:T(8,128)(2,1)S(1)} %copy-done.4), channel_id=1, replica_groups=mesh['dp'=4,'expert'=64] {'dp'}, dimensions={1}, use_global_device_ids=true | all-gather | bytes 655360 | tf_op jit(solution)/shard_map/all_gather | solution.py:168
  450.3 0.7 constant_dynamic-slice_fusion
  451.0 10.1 %reduce-scatter.3.cloned.1.call-done = f32[2,16,768]{2,1,0:T(8,128)} async-done(((f32[2,64,768]{2,1,0:T(8,128)}), f32[2,16,768]{2,1,0:T(8,128)}) %reduce-scatter.3.cloned.1.call-update) | async-done | bytes 98320 | tf_op jit(solution)/shard_map/reduce_scatter | solution.py:161
  461.0 1.7 fusion.41
  462.8 10.7 %all_gather.14 = bf16[2,64,768]{2,1,0:T(8,128)(2,1)S(1)} all-gather(bf16[2,16,768]{2,1,0:T(8,128)(2,1)S(1)} %get-tuple-element.13), channel_id=1, replica_groups=mesh['dp'=4,'expert'=64] {'dp'}, dimensions={1}, use_global_device_ids=true | all-gather | bytes 245760 | tf_op jit(solution)/shard_map/all_gather | solution.py:167
  473.4 0.6 constant_dynamic-slice_fusion.1
  474.1 35.7 %all-to-all-done.5 = bf16[4,64,3,2048]{3,0,2,1:T(4,128)(2,1)} async-done(((bf16[4,64,3,2048]{3,0,2,1:T(4,128)(2,1)}), bf16[4,64,3,2048]{3,0,2,1:T(4,128)(2,1)}, u32[]{:S(2)}, u32[]{:S(2)}) %all-to-all-start.5) | async-done | bytes 3145760 | tf_op jit(solution)/shard_map/all_to_all | solution.py:146
  509.8 6.5 %copy.66 = bf16[4,64,3,2048]{3,2,1,0:T(4,128)(2,1)} copy(bf16[4,64,3,2048]{3,0,2,1:T(4,128)(2,1)} %all-to-all-done.5) | data formatting | bytes 6291456 | tf_op jit(solution)/shard_map/all_to_all | solution.py:146
  516.3 8.8 %reshape.239 = bf16[768,2048]{1,0:T(8,128)(2,1)} reshape(bf16[4,64,3,2048]{3,2,1,0:T(4,128)(2,1)} %copy.66) | data formatting | bytes 6291456 | tf_op jit(solution)/shard_map/reshape | solution.py:153
  525.1 5.6 %gather_fusion.3 = bf16[256,2048]{1,0:T(8,128)(2,1)} fusion(bf16[768,2048]{1,0:T(8,128)(2,1)} %reshape.239, s32[1024]{0:T(1024)S(1)} %pad_clamp_fusion), kind=kCustom, calls=%fused_computation.3 | custom fusion | bytes 2098176 | tf_op jit(solution)/shard_map/jit(_take)/gather | solution.py:153
  530.8 2.4 fusion.12
  (66 shorter events, 3.9 us)
Async XLA Ops:
  7.2 303.6 %copy-start = (bf16[1,2048,768]{2,1,0:T(8,128)(2,1)S(1)}, bf16[1,2048,768]{2,1,0:T(8,128)(2,1)}, u32[]{:S(2)}) copy-start(bf16[1,2048,768]{2,1,0:T(8,128)(2,1)} %param.20) | copy-start | bytes 9437188
  7.2 9.4 %copy-start.1 = (bf16[32,2048]{1,0:T(8,128)(2,1)S(1)}, bf16[32,2048]{1,0:T(8,128)(2,1)}, u32[]{:S(2)}) copy-start(bf16[32,2048]{1,0:T(8,128)(2,1)} %param.14) | copy-start | bytes 393220
  11.4 0.6 copy-start.6
  13.9 7.0 %copy-start.8 = (s32[256]{0:T(256)}, s32[256]{0:T(256)S(1)}, u32[]{:S(2)}) copy-start(s32[256]{0:T(256)S(1)} %broadcast_multiply_fusion.2) | copy-start | bytes 3076
  14.6 0.6 copy-start.11
  38.3 6.4 %copy-start.10 = (f32[32,8]{0,1:T(8,128)S(1)}, f32[32,8]{0,1:T(8,128)}, u32[]{:S(2)}) copy-start(f32[32,8]{0,1:T(8,128)} %param.16) | copy-start | bytes 3076
  38.3 40.7 %all-to-all-start.2 = ((bf16[4,64,3,2048]{3,1,2,0:T(8,128)(2,1)}), bf16[4,64,3,2048]{3,1,2,0:T(8,128)(2,1)}, u32[]{:S(2)}, u32[]{:S(2)}) async-start(bf16[4,64,3,2048]{3,1,2,0:T(8,128)(2,1)} %copy.61), calls=%async_computation.2 | async-start | bytes 6291456 | tf_op jit(solution)/shard_map/all_to_all | solution.py:96
  79.0 38.8 %all-to-all-start = ((bf16[4,64,3,2048]{3,1,2,0:T(8,128)(2,1)}), bf16[4,64,3,2048]{3,1,2,0:T(8,128)(2,1)}, u32[]{:S(2)}, u32[]{:S(2)}) async-start(bf16[4,64,3,2048]{3,1,2,0:T(8,128)(2,1)} %copy.58), calls=%async_computation | async-start | bytes 6291456 | tf_op jit(solution)/shard_map/all_to_all | solution.py:103
  117.8 92.3 %all-to-all-start.3 = ((bf16[4,64,3,2048]{3,0,2,1:T(4,128)(2,1)}), bf16[4,64,3,2048]{3,0,2,1:T(4,128)(2,1)}, u32[]{:S(2)}, u32[]{:S(2)}) async-start(bf16[4,64,3,2048]{3,0,2,1:T(4,128)(2,1)} %copy.62), calls=%async_computation.3 | async-start | bytes 6291456 | tf_op jit(solution)/shard_map/all_to_all | solution.py:95
  142.8 75.5 %copy-start.5 = (f32[2,16,768]{2,1,0:T(8,128)S(1)}, f32[2,16,768]{2,1,0:T(8,128)}, u32[]{:S(2)}) copy-start(f32[2,16,768]{2,1,0:T(8,128)} %param.22) | copy-start | bytes 294916
  210.1 79.7 %all-to-all-start.1 = ((bf16[4,64,3,2048]{3,0,2,1:T(4,128)(2,1)}), bf16[4,64,3,2048]{3,0,2,1:T(4,128)(2,1)}, u32[]{:S(2)}, u32[]{:S(2)}) async-start(bf16[4,64,3,2048]{3,0,2,1:T(4,128)(2,1)} %copy.59), calls=%async_computation.1 | async-start | bytes 6291456 | tf_op jit(solution)/shard_map/all_to_all | solution.py:102
  216.4 125.2 %reduce-scatter.5.cloned.1.call-start = ((), (), s32[]{:S(2)}) async-start(), calls=%async_computation.9 | async-start | bytes 1310720 | tf_op jit(solution)/shard_map/reduce_scatter | solution.py:162
  228.8 90.7 %copy-start.13 = (f32[2]{0:T(128)}, f32[2]{0:T(128)S(1)}, u32[]{:S(2)}) copy-start(f32[2]{0:T(128)S(1)} %compare_convert_fusion) | copy-start | bytes 28
  305.2 5.6 %copy-start.2 = (bf16[768,2048]{1,0:T(8,128)(2,1)S(1)}, bf16[768,2048]{1,0:T(8,128)(2,1)}, u32[]{:S(2)}) copy-start(bf16[768,2048]{1,0:T(8,128)(2,1)} %reshape.237) | copy-start | bytes 9437188
  310.8 4.5 copy-start.16
  343.9 14.3 %copy-start.3 = (f32[768,768]{1,0:T(8,128)S(1)}, f32[768,768]{1,0:T(8,128)}, u32[]{:S(2)}) copy-start(f32[768,768]{1,0:T(8,128)} %fusion.7) | copy-start | bytes 7077892
  355.1 3.6 copy-start.17
  355.1 3.6 copy-start.18
  358.2 1.9 copy-start.15
  421.4 16.6 %copy-start.14 = (f32[2]{0:T(128)S(1)}, f32[2]{0:T(128)}, u32[]{:S(2)}) copy-start(f32[2]{0:T(128)} %copy-done.13) | copy-start | bytes 28
  421.4 17.5 %copy-start.9 = (s32[256]{0:T(256)S(1)}, s32[256]{0:T(256)}, u32[]{:S(2)}) copy-start(s32[256]{0:T(256)} %copy-done.8) | copy-start | bytes 3076
  421.4 17.6 %copy-start.7 = (s32[256]{0:T(256)S(1)}, s32[256]{0:T(256)}, u32[]{:S(2)}) copy-start(s32[256]{0:T(256)} %convert_reduce_fusion) | copy-start | bytes 3076
  421.4 17.7 %copy-start.12 = (s32[256,1]{0,1:T(1,128)S(1)}, s32[256,1]{0,1:T(1,128)}, u32[]{:S(2)}) copy-start(s32[256,1]{0,1:T(1,128)} %copy-done.11) | copy-start | bytes 3076
  421.4 17.8 %copy-start.4 = (bf16[2,16,2048]{2,1,0:T(8,128)(2,1)S(1)}, bf16[2,16,2048]{2,1,0:T(8,128)(2,1)}, u32[]{:S(2)}) copy-start(bf16[2,16,2048]{2,1,0:T(8,128)(2,1)} %get-tuple-element.9) | copy-start | bytes 393220
  421.4 88.4 %all-to-all-start.5 = ((bf16[4,64,3,2048]{3,0,2,1:T(4,128)(2,1)}), bf16[4,64,3,2048]{3,0,2,1:T(4,128)(2,1)}, u32[]{:S(2)}, u32[]{:S(2)}) async-start(bf16[4,64,3,2048]{3,0,2,1:T(4,128)(2,1)} %copy.65), calls=%async_computation.5 | async-start | bytes 6291456 | tf_op jit(solution)/shard_map/all_to_all | solution.py:146
  436.3 24.7 %reduce-scatter.3.cloned.1.call-start = ((), (), s32[]{:S(2)}) async-start(), calls=%async_computation.8 | async-start | bytes 491520 | tf_op jit(solution)/shard_map/reduce_scatter | solution.py:161
Sparse Core Ops, SparseCore 0:
  321.9 19.6 reduce-scatter.4
  439.9 21.1 reduce-scatter.2
where the time goes:
time: 549 us; the launch traced here: 540 us
  waiting for transfers between devices  207 us (38%)
  local copies, waits for them, and re-layouts  131 us (24%)
  blocking collectives  79.6 us (14%)
  starting transfers between devices  50.2 us (9%)
  matrix products  33.8 us (6%)
  other arithmetic  24 us (4%)
  between operations  15.5 us (3%)
    all_to_all x1, waiting for transfers between devices, per_device(): lax.all_to_all(lax.all_to_all(send_input, 'dp', split_axis=0, concat_axis...  67.2 us
    all_to_all x1, waiting for transfers between devices, per_device(): lax.all_to_all(lax.all_to_all(send_grad, 'dp', split_axis=0, concat_axis=...  45.5 us
    all_to_all x1, blocking collectives, per_device(): lax.all_to_all(back_block, 'dp', split_axis=0, concat_axis=0, tiled=True)  36.2 us
    all_to_all x1, waiting for transfers between devices, per_device(): lax.all_to_all(lax.all_to_all(back_block, 'dp', split_axis=0, concat_axis...  35.7 us
    all_to_all x1, waiting for transfers between devices, per_device(): lax.all_to_all(send_grad, 'dp', split_axis=0, concat_axis=0, tiled=True)  28.1 us
    dot_general x6, matrix products, contract_product(): lax.dot_general(left, right, (((left_dim,), (right_dim,)), ((), ())), pre...  23.2 us
    all_to_all x1, starting transfers between devices, per_device(): lax.all_to_all(lax.all_to_all(send_input, 'dp', split_axis=0, concat_axis...  19.1 us
    gather x2, local copies, waits for them, and re-layouts, pack_rows(): send_grad = jnp.take(scaled, filler, axis=0, mode='fill', fill_value=0)  17.6 us
  transfers between devices with their start and end apart: 7, of which 7 were waited for; matrix products, arithmetic and copies ran while one was open for 13% of the time, Pallas kernels for 0%

commit v1 on v0

--- a/solution.py
+++ b/solution.py
@@ -9,6 +9,22 @@
 beta_two = 0.999
 decay_rate = 0.01
 adam_eps = 1e-08
+
+
+def ring_gather(x, axis, dim):
+    ways, here, step = (lax.axis_size(axis), lax.axis_index(axis), x.shape[dim])
+    dims = [n * ways if d == dim else n for d, n in enumerate(x.shape)]
+    full = lax.dynamic_update_slice_in_dim(jnp.zeros(dims, x.dtype), x, here * step, axis=dim)
+    going_up = going_down = x
+    for far in range(1, ways // 2 + 1):
+        going_up = lax.ppermute(going_up, axis, [(d, (d + 1) % ways) for d in range(ways)])
+        full = lax.dynamic_update_slice_in_dim(full, going_up, (here - far) % ways * step, axis=dim)
+        if 2 * far < ways:
+            going_down = lax.ppermute(going_down, axis, [(d, (d - 1) % ways) for d in range(ways)])
+            full = lax.dynamic_update_slice_in_dim(
+                full, going_down, (here + far) % ways * step, axis=dim
+            )
+    return full
 
 
 def contract_product(left, right, left_dim, right_dim):
@@ -165,7 +181,7 @@
     step_out, momentum_out, variance_out = adamw(adapter_out, summed_out, moment_out, second_out)
     copied_in, copied_out = (
         lax.all_gather(step_in.astype(jnp.bfloat16), "dp", axis=1, tiled=True),
-        lax.all_gather(step_out.astype(jnp.bfloat16), "dp", axis=1, tiled=True),
+        ring_gather(step_out.astype(jnp.bfloat16), "dp", 1),
     )
     replica_in = lax.dynamic_index_in_dim(copied_in, hosted_local, 0, keepdims=True)
     replica_out = lax.dynamic_index_in_dim(copied_out, hosted_local, 0, keepdims=True)

time: 549 us -> 539 us (0.982)
  blocking collectives: 79.6 us -> 67.9 us
    all_to_all x1, waiting for transfers between devices: 35.7 us -> 20.5 us  [per_device(): lax.all_to_all(lax.all_to_all(back_block, 'dp', split_axis=0, concat_axis...]
    all_gather x1 -> x0, blocking collectives: 11.1 us -> none  [per_device(): lax.all_gather(step_out.astype(jnp.bfloat16), 'dp', axis=1, tiled=True)]
    reduce_scatter x1, waiting for transfers between devices: 12.9 us -> 23.7 us  [per_device(): lax.psum_scatter(placed_out, 'dp', scatter_dimension=1, tiled=True)]
  transfers between devices with their start and end apart: 7 -> 10, of which waited for: 7 -> 9; matrix products, arithmetic and copies ran while one was open for 13% -> 14% of each run, Pallas kernels for 0% -> 0%
where the time goes in v1:
time: 539 us; the launch traced here: 530 us
  waiting for transfers between devices  205 us (38%)
  local copies, waits for them, and re-layouts  129 us (24%)
  blocking collectives  67.9 us (13%)
  starting transfers between devices  53.8 us (10%)
  matrix products  33.7 us (6%)
  other arithmetic  24.7 us (5%)
  between operations  15.6 us (3%)
    all_to_all x1, waiting for transfers between devices, per_device(): lax.all_to_all(lax.all_to_all(send_input, 'dp', split_axis=0, concat_axis...  67.2 us
    all_to_all x1, waiting for transfers between devices, per_device(): lax.all_to_all(lax.all_to_all(send_grad, 'dp', split_axis=0, concat_axis=...  43.6 us
    all_to_all x1, blocking collectives, per_device(): lax.all_to_all(back_block, 'dp', split_axis=0, concat_axis=0, tiled=True)  35 us
    all_to_all x1, waiting for transfers between devices, per_device(): lax.all_to_all(send_grad, 'dp', split_axis=0, concat_axis=0, tiled=True)  28.2 us
    reduce_scatter x1, waiting for transfers between devices, per_device(): lax.psum_scatter(placed_out, 'dp', scatter_dimension=1, tiled=True)  23.7 us
    dot_general x6, matrix products, contract_product(): lax.dot_general(left, right, (((left_dim,), (right_dim,)), ((), ())), pre...  21.7 us
    all_to_all x1, waiting for transfers between devices, per_device(): lax.all_to_all(lax.all_to_all(back_block, 'dp', split_axis=0, concat_axis...  20.5 us
    all_to_all x1, starting transfers between devices, per_device(): lax.all_to_all(lax.all_to_all(send_input, 'dp', split_axis=0, concat_axis...  19.1 us
  transfers between devices with their start and end apart: 10, of which 9 were waited for; matrix products, arithmetic and copies ran while one was open for 14% of the time, Pallas kernels for 0%

profile of v1, /device:TPU:1, one launch (start us, length us, event | category | flops | bytes accessed | tf_op | source)
XLA Modules:
  0.0 530.1 jit_solution(3820169630055768124)
XLA Ops:
  7.2 0.9 copy.50
  8.3 0.7 convert_reduce_fusion
  9.7 0.8 copy.52
  10.4 0.7 gather_fusion
  12.0 0.7 and_select_fusion.1
  12.9 1.0 multiply_reduce_fusion
  13.9 0.7 compare_select_fusion.2
  15.1 1.4 scatter_custom_fusion
  16.6 4.2 gather_fusion.2
  20.8 9.1 %gather.26 = bf16[4,64,3,2048]{3,2,1,0:T(4,128)(2,1)} reshape(bf16[768,2048]{1,0:T(8,128)(2,1)} %gather_fusion.2) | data formatting | bytes 6291456 | tf_op jit(solution)/shard_map/jit(_take)/gather | solution.py:55
  30.2 4.1 broadcast_select_fusion
  34.3 4.0 copy.61
  38.3 5.2 all-to-all-start.2
  43.7 0.9 convert_element_type.56
  44.9 1.2 fusion.9
  46.0 8.5 %gather_fusion.1 = bf16[768,2048]{1,0:T(8,128)(2,1)} fusion(bf16[256,2048]{1,0:T(8,128)(2,1)} %fusion.9, s32[1024]{0:T(1024)S(1)} %pad_clamp_fusion.2), kind=kCustom, calls=%fused_computation.1 | custom fusion | bytes 6294528 | tf_op jit(solution)/shard_map/jit(_take)/gather | solution.py:56
  54.5 9.1 %gather.24 = bf16[4,64,3,2048]{3,2,1,0:T(4,128)(2,1)} reshape(bf16[768,2048]{1,0:T(8,128)(2,1)} %gather_fusion.1) | data formatting | bytes 6291456 | tf_op jit(solution)/shard_map/jit(_take)/gather | solution.py:56
  63.6 4.1 broadcast_select_fusion.1
  67.7 4.0 copy.58
  71.8 7.2 %all-to-all-done.2 = bf16[4,64,3,2048]{3,1,2,0:T(8,128)(2,1)} async-done(((bf16[4,64,3,2048]{3,1,2,0:T(8,128)(2,1)}), bf16[4,64,3,2048]{3,1,2,0:T(8,128)(2,1)}, u32[]{:S(2)}, u32[]{:S(2)}) %all-to-all-start.2) | async-done | bytes 3145760 | tf_op jit(solution)/shard_map/all_to_all | solution.py:112
  78.9 4.7 all-to-all-start
  83.6 6.0 %copy.62 = bf16[4,64,3,2048]{3,0,2,1:T(4,128)(2,1)} copy(bf16[4,64,3,2048]{3,1,2,0:T(8,128)(2,1)} %all-to-all-done.2) | data formatting | bytes 6291456 | tf_op jit(solution)/shard_map/all_to_all | solution.py:112
  89.6 28.2 %all-to-all-done = bf16[4,64,3,2048]{3,1,2,0:T(8,128)(2,1)} async-done(((bf16[4,64,3,2048]{3,1,2,0:T(8,128)(2,1)}), bf16[4,64,3,2048]{3,1,2,0:T(8,128)(2,1)}, u32[]{:S(2)}, u32[]{:S(2)}) %all-to-all-start) | async-done | bytes 3145760 | tf_op jit(solution)/shard_map/all_to_all | solution.py:119
  117.8 19.1 %all-to-all-start.3 = ((bf16[4,64,3,2048]{3,0,2,1:T(4,128)(2,1)}), bf16[4,64,3,2048]{3,0,2,1:T(4,128)(2,1)}, u32[]{:S(2)}, u32[]{:S(2)}) async-start(bf16[4,64,3,2048]{3,0,2,1:T(4,128)(2,1)} %copy.62), calls=%async_computation.3 | async-start | bytes 6291456 | tf_op jit(solution)/shard_map/all_to_all | solution.py:111
  136.8 6.0 %copy.59 = bf16[4,64,3,2048]{3,0,2,1:T(4,128)(2,1)} copy(bf16[4,64,3,2048]{3,1,2,0:T(8,128)(2,1)} %all-to-all-done) | data formatting | bytes 6291456 | tf_op jit(solution)/shard_map/all_to_all | solution.py:119
  142.8 67.2 %all-to-all-done.3 = bf16[4,64,3,2048]{3,0,2,1:T(4,128)(2,1)} async-done(((bf16[4,64,3,2048]{3,0,2,1:T(4,128)(2,1)}), bf16[4,64,3,2048]{3,0,2,1:T(4,128)(2,1)}, u32[]{:S(2)}, u32[]{:S(2)}) %all-to-all-start.3) | async-done | bytes 3145760 | tf_op jit(solution)/shard_map/all_to_all | solution.py:111
  210.1 6.3 %all-to-all-start.1 = ((bf16[4,64,3,2048]{3,0,2,1:T(4,128)(2,1)}), bf16[4,64,3,2048]{3,0,2,1:T(4,128)(2,1)}, u32[]{:S(2)}, u32[]{:S(2)}) async-start(bf16[4,64,3,2048]{3,0,2,1:T(4,128)(2,1)} %copy.59), calls=%async_computation.1 | async-start | bytes 6291456 | tf_op jit(solution)/shard_map/all_to_all | solution.py:118
  216.4 1.3 dynamic_slice.19
  219.0 11.7 %all_gather.9 = bf16[2,64,2048]{2,1,0:T(8,128)(2,1)} all-gather(bf16[2,16,2048]{2,1,0:T(8,128)(2,1)} %convert_element_type.58), channel_id=1, replica_groups=mesh['dp'=4,'expert'=64] {'dp'}, dimensions={1}, use_global_device_ids=true | all-gather | bytes 655360 | tf_op jit(solution)/shard_map/all_gather | solution.py:128
  230.7 6.5 %copy.63 = bf16[4,64,3,2048]{3,2,1,0:T(4,128)(2,1)} copy(bf16[4,64,3,2048]{3,0,2,1:T(4,128)(2,1)} %all-to-all-done.3) | data formatting | bytes 6291456 | tf_op jit(solution)/shard_map/all_to_all | solution.py:111
  237.3 9.0 %reshape.237 = bf16[768,2048]{1,0:T(8,128)(2,1)} reshape(bf16[4,64,3,2048]{3,2,1,0:T(4,128)(2,1)} %copy.63) | data formatting | bytes 6291456 | tf_op jit(solution)/shard_map/reshape | solution.py:133
  246.3 43.6 %all-to-all-done.1 = bf16[4,64,3,2048]{3,0,2,1:T(4,128)(2,1)} async-done(((bf16[4,64,3,2048]{3,0,2,1:T(4,128)(2,1)}), bf16[4,64,3,2048]{3,0,2,1:T(4,128)(2,1)}, u32[]{:S(2)}, u32[]{:S(2)}) %all-to-all-start.1) | async-done | bytes 3145760 | tf_op jit(solution)/shard_map/all_to_all | solution.py:118
  289.8 6.5 %copy.60 = bf16[4,64,3,2048]{3,2,1,0:T(4,128)(2,1)} copy(bf16[4,64,3,2048]{3,0,2,1:T(4,128)(2,1)} %all-to-all-done.1) | data formatting | bytes 6291456 | tf_op jit(solution)/shard_map/all_to_all | solution.py:118
  296.3 8.8 %reshape.236 = bf16[768,2048]{1,0:T(8,128)(2,1)} reshape(bf16[4,64,3,2048]{3,2,1,0:T(4,128)(2,1)} %copy.60) | data formatting | bytes 6291456 | tf_op jit(solution)/shard_map/reshape | solution.py:134
  305.2 5.6 %fusion.2 = f32[768,768]{1,0:T(8,128)S(1)} fusion(bf16[768,2048]{1,0:T(8,128)(2,1)} %reshape.237, bf16[1,2048,768]{2,1,0:T(8,128)(2,1)} %param.19), kind=kOutput, calls=%fused_computation.10 | convolution fusion | flops 2415919104 | bytes 8650752 | tf_op jit(solution)/shard_map/dot_general | solution.py:138
  310.8 4.2 multiply_convert_fusion
  315.0 1.1 convolution_convert_fusion.1
  316.4 0.9 broadcast_multiply_fusion.1
  317.3 6.9 %fusion.7 = f32[768,768]{1,0:T(8,128)} fusion(bf16[768,2048]{1,0:T(8,128)(2,1)} %reshape.236, bf16[1,768,2048]{2,1,0:T(8,128)(2,1)} %param.21), kind=kOutput, calls=%fused_computation.15 | convolution fusion | flops 2415919104 | bytes 8650752 | tf_op jit(solution)/shard_map/dot_general | solution.py:31
  324.2 9.5 %reduce-scatter.3.cloned.1.call-done = f32[2,16,768]{2,1,0:T(8,128)} async-done(((f32[2,64,768]{2,1,0:T(8,128)}), f32[2,16,768]{2,1,0:T(8,128)}) %reduce-scatter.3.cloned.1.call-update) | async-done | bytes 98320 | tf_op jit(solution)/shard_map/reduce_scatter | solution.py:177
  333.7 2.0 fusion.40
  335.7 10.1 %all_gather.10 = bf16[2,64,768]{2,1,0:T(8,128)(2,1)S(1)} all-gather(bf16[2,16,768]{2,1,0:T(8,128)(2,1)S(1)} %get-tuple-element.24), channel_id=1, replica_groups=mesh['dp'=4,'expert'=64] {'dp'}, dimensions={1}, use_global_device_ids=true | all-gather | bytes 245760 | tf_op jit(solution)/shard_map/all_gather | solution.py:127
  345.7 2.2 multiply_add_fusion
  348.0 5.0 fusion
  352.9 4.2 add_convert_fusion
  357.1 9.1 %reshape.238 = bf16[4,64,3,2048]{3,2,1,0:T(4,128)(2,1)} reshape(bf16[768,2048]{1,0:T(8,128)(2,1)} %add_convert_fusion) | data formatting | bytes 6291456 | tf_op jit(solution)/shard_map/reshape | solution.py:161
  366.2 4.5 copy.64
  370.7 35.0 %all_to_all.30 = bf16[4,64,3,2048]{3,1,2,0:T(8,128)(2,1)S(1)} all-to-all(bf16[4,64,3,2048]{3,1,2,0:T(8,128)(2,1)S(1)} %copy.64), channel_id=1, replica_groups=mesh['dp'=4,'expert'=64] {'dp'}, dimensions={0} | all-to-all | bytes 6291456 | tf_op jit(solution)/shard_map/all_to_all | solution.py:163
  405.7 4.1 copy.65
  409.8 16.3 %all-to-all-start.5 = ((bf16[4,64,3,2048]{3,0,2,1:T(4,128)(2,1)}), bf16[4,64,3,2048]{3,0,2,1:T(4,128)(2,1)}, u32[]{:S(2)}, u32[]{:S(2)}) async-start(bf16[4,64,3,2048]{3,0,2,1:T(4,128)(2,1)} %copy.65), calls=%async_computation.5 | async-start | bytes 6291456 | tf_op jit(solution)/shard_map/all_to_all | solution.py:162
  426.1 4.3 convolution_multiply_fusion
  430.4 2.2 broadcast_multiply_fusion
  432.9 23.7 %reduce-scatter.5.cloned.1.call-done = f32[2,16,2048]{2,1,0:T(8,128)} async-done(((f32[2,64,2048]{2,1,0:T(8,128)}), f32[2,16,2048]{2,1,0:T(8,128)}) %reduce-scatter.5.cloned.1.call-update) | async-done | bytes 262160 | tf_op jit(solution)/shard_map/reduce_scatter | solution.py:178
  456.7 2.1 constant_dynamic-update-slice_fusion.3
  459.0 11.1 %all_gather.11 = bf16[2,64,768]{2,1,0:T(8,128)(2,1)S(1)} all-gather(bf16[2,16,768]{2,1,0:T(8,128)(2,1)S(1)} %copy-done.9), channel_id=1, replica_groups=mesh['dp'=4,'expert'=64] {'dp'}, dimensions={1}, use_global_device_ids=true | all-gather | bytes 245760 | tf_op jit(solution)/shard_map/all_gather | solution.py:183
  470.8 2.0 collective-permute-start.1
  472.8 1.9 collective-permute-done.1
  474.7 3.5 collective-permute-done.2
  478.2 0.7 constant_dynamic-slice_fusion
  478.9 20.5 %all-to-all-done.5 = bf16[4,64,3,2048]{3,0,2,1:T(4,128)(2,1)} async-done(((bf16[4,64,3,2048]{3,0,2,1:T(4,128)(2,1)}), bf16[4,64,3,2048]{3,0,2,1:T(4,128)(2,1)}, u32[]{:S(2)}, u32[]{:S(2)}) %all-to-all-start.5) | async-done | bytes 3145760 | tf_op jit(solution)/shard_map/all_to_all | solution.py:162
  499.5 6.5 %copy.66 = bf16[4,64,3,2048]{3,2,1,0:T(4,128)(2,1)} copy(bf16[4,64,3,2048]{3,0,2,1:T(4,128)(2,1)} %all-to-all-done.5) | data formatting | bytes 6291456 | tf_op jit(solution)/shard_map/all_to_all | solution.py:162
  506.0 8.8 %reshape.239 = bf16[768,2048]{1,0:T(8,128)(2,1)} reshape(bf16[4,64,3,2048]{3,2,1,0:T(4,128)(2,1)} %copy.66) | data formatting | bytes 6291456 | tf_op jit(solution)/shard_map/reshape | solution.py:169
  514.8 5.6 %gather_fusion.3 = bf16[256,2048]{1,0:T(8,128)(2,1)} fusion(bf16[768,2048]{1,0:T(8,128)(2,1)} %reshape.239, s32[1024]{0:T(1024)S(1)} %pad_clamp_fusion), kind=kCustom, calls=%fused_computation.3 | custom fusion | bytes 2098176 | tf_op jit(solution)/shard_map/jit(_take)/gather | solution.py:169
  520.4 2.4 fusion.12
  (71 shorter events, 5.4 us)
Async XLA Ops:
  7.2 303.6 %copy-start = (bf16[1,2048,768]{2,1,0:T(8,128)(2,1)S(1)}, bf16[1,2048,768]{2,1,0:T(8,128)(2,1)}, u32[]{:S(2)}) copy-start(bf16[1,2048,768]{2,1,0:T(8,128)(2,1)} %param.20) | copy-start | bytes 9437188
  7.2 9.4 %copy-start.1 = (bf16[32,2048]{1,0:T(8,128)(2,1)S(1)}, bf16[32,2048]{1,0:T(8,128)(2,1)}, u32[]{:S(2)}) copy-start(bf16[32,2048]{1,0:T(8,128)(2,1)} %param.14) | copy-start | bytes 393220
  11.4 0.6 copy-start.8
  14.6 0.6 copy-start.12
  38.3 6.4 %copy-start.11 = (f32[32,8]{0,1:T(8,128)S(1)}, f32[32,8]{0,1:T(8,128)}, u32[]{:S(2)}) copy-start(f32[32,8]{0,1:T(8,128)} %param.16) | copy-start | bytes 3076
  38.3 40.7 %all-to-all-start.2 = ((bf16[4,64,3,2048]{3,1,2,0:T(8,128)(2,1)}), bf16[4,64,3,2048]{3,1,2,0:T(8,128)(2,1)}, u32[]{:S(2)}, u32[]{:S(2)}) async-start(bf16[4,64,3,2048]{3,1,2,0:T(8,128)(2,1)} %copy.61), calls=%async_computation.2 | async-start | bytes 6291456 | tf_op jit(solution)/shard_map/all_to_all | solution.py:112
  78.9 38.8 %all-to-all-start = ((bf16[4,64,3,2048]{3,1,2,0:T(8,128)(2,1)}), bf16[4,64,3,2048]{3,1,2,0:T(8,128)(2,1)}, u32[]{:S(2)}, u32[]{:S(2)}) async-start(bf16[4,64,3,2048]{3,1,2,0:T(8,128)(2,1)} %copy.58), calls=%async_computation | async-start | bytes 6291456 | tf_op jit(solution)/shard_map/all_to_all | solution.py:119
  117.8 92.3 %all-to-all-start.3 = ((bf16[4,64,3,2048]{3,0,2,1:T(4,128)(2,1)}), bf16[4,64,3,2048]{3,0,2,1:T(4,128)(2,1)}, u32[]{:S(2)}, u32[]{:S(2)}) async-start(bf16[4,64,3,2048]{3,0,2,1:T(4,128)(2,1)} %copy.62), calls=%async_computation.3 | async-start | bytes 6291456 | tf_op jit(solution)/shard_map/all_to_all | solution.py:111
  142.8 75.5 %copy-start.6 = (f32[2,16,2048]{2,1,0:T(8,128)S(1)}, f32[2,16,2048]{2,1,0:T(8,128)}, u32[]{:S(2)}) copy-start(f32[2,16,2048]{2,1,0:T(8,128)} %param.23) | copy-start | bytes 786436
  210.1 79.7 %all-to-all-start.1 = ((bf16[4,64,3,2048]{3,0,2,1:T(4,128)(2,1)}), bf16[4,64,3,2048]{3,0,2,1:T(4,128)(2,1)}, u32[]{:S(2)}, u32[]{:S(2)}) async-start(bf16[4,64,3,2048]{3,0,2,1:T(4,128)(2,1)} %copy.59), calls=%async_computation.1 | async-start | bytes 6291456 | tf_op jit(solution)/shard_map/all_to_all | solution.py:118
  216.4 117.3 %reduce-scatter.3.cloned.1.call-start = ((), (), s32[]{:S(2)}) async-start(), calls=%async_computation.8 | async-start | bytes 491520 | tf_op jit(solution)/shard_map/reduce_scatter | solution.py:177
  305.2 5.6 %copy-start.4 = (bf16[768,2048]{1,0:T(8,128)(2,1)S(1)}, bf16[768,2048]{1,0:T(8,128)(2,1)}, u32[]{:S(2)}) copy-start(bf16[768,2048]{1,0:T(8,128)(2,1)} %reshape.237) | copy-start | bytes 9437188
  310.8 4.2 copy-start.15
  310.8 4.2 copy-start.2
  310.8 4.2 copy-start.5
  315.0 1.4 copy-start.3
  333.7 14.3 %copy-start.14 = (bf16[1,2048,768]{2,1,0:T(8,128)(2,1)S(1)}, bf16[1,2048,768]{2,1,0:T(8,128)(2,1)}, u32[]{:S(2)}) copy-start(bf16[1,2048,768]{2,1,0:T(8,128)(2,1)} %param.19) | copy-start | bytes 9437188
  333.7 14.3 %copy-start.16 = (f32[768,768]{1,0:T(8,128)S(1)}, f32[768,768]{1,0:T(8,128)}, u32[]{:S(2)}) copy-start(f32[768,768]{1,0:T(8,128)} %copy-done.15) | copy-start | bytes 7077892
  345.7 7.2 %copy-start.7 = (bf16[2,64,768]{2,1,0:T(8,128)(2,1)}, bf16[2,64,768]{2,1,0:T(8,128)(2,1)S(1)}, u32[]{:S(2)}) copy-start(bf16[2,64,768]{2,1,0:T(8,128)(2,1)S(1)} %all_gather.10) | copy-start | bytes 589828
  409.8 89.7 %all-to-all-start.5 = ((bf16[4,64,3,2048]{3,0,2,1:T(4,128)(2,1)}), bf16[4,64,3,2048]{3,0,2,1:T(4,128)(2,1)}, u32[]{:S(2)}, u32[]{:S(2)}) async-start(bf16[4,64,3,2048]{3,0,2,1:T(4,128)(2,1)} %copy.65), calls=%async_computation.5 | async-start | bytes 6291456 | tf_op jit(solution)/shard_map/all_to_all | solution.py:162
  426.0 6.8 %copy-start.10 = (s32[256]{0:T(256)S(1)}, s32[256]{0:T(256)}, u32[]{:S(2)}) copy-start(s32[256]{0:T(256)} %convert_reduce_fusion) | copy-start | bytes 3076
  426.0 6.8 %copy-start.13 = (s32[256,1]{0,1:T(1,128)S(1)}, s32[256,1]{0,1:T(1,128)}, u32[]{:S(2)}) copy-start(s32[256,1]{0,1:T(1,128)} %copy-done.12) | copy-start | bytes 3076
  426.0 30.6 %reduce-scatter.5.cloned.1.call-start = ((), (), s32[]{:S(2)}) async-start(), calls=%async_computation.9 | async-start | bytes 1310720 | tf_op jit(solution)/shard_map/reduce_scatter | solution.py:178
  430.4 28.6 %copy-start.9 = (bf16[2,16,768]{2,1,0:T(8,128)(2,1)S(1)}, bf16[2,16,768]{2,1,0:T(8,128)(2,1)}, u32[]{:S(2)}) copy-start(bf16[2,16,768]{2,1,0:T(8,128)(2,1)} %get-tuple-element.14) | copy-start | bytes 147460
  458.8 14.0 %collective-permute-start = (bf16[2,16,2048]{2,1,0:T(8,128)(2,1)S(1)}, bf16[2,16,2048]{2,1,0:T(8,128)(2,1)S(1)}, u32[]{:S(2)}, u32[]{:S(2)}) collective-permute-start(bf16[2,16,2048]{2,1,0:T(8,128)(2,1)S(1)} %get-tuple-element.10), channel_id=1, source_target_pairs={{0,64},{64,128},{128,192},{192,0},{1,65},{65,129},{129,193},{193,1... | collective-permute-start | bytes 393224 | tf_op jit(solution)/shard_map/ppermute | solution.py:20
  470.8 3.9 collective-permute-start.1
  472.8 5.4 %collective-permute-start.2 = (bf16[2,16,2048]{2,1,0:T(8,128)(2,1)S(1)}, bf16[2,16,2048]{2,1,0:T(8,128)(2,1)S(1)}, u32[]{:S(2)}, u32[]{:S(2)}) collective-permute-start(bf16[2,16,2048]{2,1,0:T(8,128)(2,1)S(1)} %collective-permute-done), channel_id=1, source_target_pairs={{0,64},{64,128},{128,192},{192,0},{1,65},{65,129},{129,193},{193,1... | collective-permute-start | bytes 393224 | tf_op jit(solution)/shard_map/ppermute | solution.py:20
Sparse Core Ops, SparseCore 0:
  317.4 16.1 reduce-scatter.2
  432.7 23.8 reduce-scatter.4
